TPU v7x, 128 devices: a whole 4x4x4 slice. The times are simulated.
128 devices in a mesh: gx: 4 (over z), gy: 4 (over y), gz: 8 (over x, core).
Axes of the slice: x: 4, y: 4, z: 4, core: 2. Of those that a mesh axis runs over, the one named last changes fastest.
Arguments:
- resident_basis: bfloat16 [5, 256, 16, 32, 2048], P(None, None, 'gx', 'gy', 'gz'), may hold values from -6 to 6
- block_basis: bfloat16 [2, 5, 32, 16, 32, 2048], P(None, None, None, 'gx', 'gy', 'gz'), may hold values from -6 to 6
- jacobian: bfloat16 [7, 5, 5, 16, 32, 2048], P(None, None, None, 'gx', 'gy', 'gz'), may hold values from -1 to 1
- volumes: float32 [16, 32, 2048], P('gx', 'gy', 'gz'), may hold values from 0.5 to 2
- cell_codes: int32 [16, 32, 2048], P('gx', 'gy', 'gz'), may hold values from 0 to 2
- phase_index: int32 [1], replicated, may hold values from 0 to 23
Outputs:
- reduced_jacobian: float32 [256, 64], replicated
- reduced_mass: float32 [256, 64], replicated
All inputs are finite; a program needn't handle non-finite values.
Results may differ from a plain program's by a relative error of at most 0.0031.
Values may be sent and summed in bfloat16 or wider, within the bound.
A program may use at most 320 MiB of HBM per device.

v0:
```python
import math

import jax
import jax.numpy as jnp
from jax import lax
from jax.sharding import PartitionSpec as P

BLADES = 24


def with_halo(block, sides, width):
    for axis, dim in sides:
        count = lax.axis_size(axis)
        forward = [(i, i + 1) for i in range(count - 1)]
        forward.append((count - 1, 0))
        backward = [(target, source) for source, target in forward]
        low = lax.ppermute(
            lax.slice_in_dim(block, block.shape[dim] - width, None, axis=dim), axis, forward
        )
        high = lax.ppermute(lax.slice_in_dim(block, 0, width, axis=dim), axis, backward)
        block = jnp.concatenate([low, block, high], axis=dim)
    return block


def lower_weight(count, value):
    spots = jnp.arange(count)
    return jnp.where(spots == 0, value, 1.0)


def upper_weight(count, value):
    spots = jnp.arange(count)
    return jnp.where(spots == count - 1, value, 1.0)


def rotate_rims(padded_re, padded_im, cosine, sine, first_y, last_y):
    re_low = padded_re[:, :, :, 0, :]
    im_low = padded_im[:, :, :, 0, :]
    re_high = padded_re[:, :, :, -1, :]
    im_high = padded_im[:, :, :, -1, :]
    new_re_low = jnp.where(first_y, cosine * re_low + sine * im_low, re_low)
    new_im_low = jnp.where(first_y, cosine * im_low - sine * re_low, im_low)
    new_re_high = jnp.where(last_y, cosine * re_high - sine * im_high, re_high)
    new_im_high = jnp.where(last_y, sine * re_high + cosine * im_high, im_high)
    padded_re = padded_re.at[:, :, :, 0, :].set(new_re_low).at[:, :, :, -1, :].set(new_re_high)
    padded_im = padded_im.at[:, :, :, 0, :].set(new_im_low).at[:, :, :, -1, :].set(new_im_high)
    return [padded_re, padded_im]


def apply_block(block, padded, jacobian, penalty, edges):
    sx, sy, sz = block.shape[-3:]
    near = [
        block.astype(jnp.float32),
        padded[:, :, 0:sx, 1 : sy + 1, 1 : sz + 1],
        padded[:, :, 2 : sx + 2, 1 : sy + 1, 1 : sz + 1],
        padded[:, :, 1 : sx + 1, 0:sy, 1 : sz + 1],
        padded[:, :, 1 : sx + 1, 2 : sy + 2, 1 : sz + 1],
        padded[:, :, 1 : sx + 1, 1 : sy + 1, 0:sz],
        padded[:, :, 1 : sx + 1, 1 : sy + 1, 2 : sz + 2],
    ]
    total = -penalty * block.astype(jnp.float32)
    for spot in range(7):
        values = near[spot]
        if spot in (1, 2, 5, 6):
            values = values * edges[spot]
        for field in range(block.shape[0]):
            total = (
                total + jacobian[spot, :, field][:, None].astype(jnp.float32) * values[field][None]
            )
    return total


def project(resident_basis, weighted):
    return lax.dot_general(
        resident_basis,
        weighted,
        (((0, 2, 3, 4), (0, 2, 3, 4)), ((), ())),
        preferred_element_type=jnp.float32,
    )


def block_terms(block, padded, resident_basis, jacobian, volumes, penalty, edges):
    applied = apply_block(block, padded, jacobian, penalty, edges)
    weighted = (volumes * applied).astype(jnp.bfloat16)
    massed = (volumes * block.astype(jnp.float32)).astype(jnp.bfloat16)
    return (project(resident_basis, weighted), project(resident_basis, massed))


def shards(resident_basis, block_basis, jacobian, volumes, cell_codes, phase_index):
    sigma = 2.0 * math.pi * phase_index[0].astype(jnp.float32) / BLADES
    cosine = jnp.cos(sigma)
    sine = jnp.sin(sigma)
    sx, sy, sz = volumes.shape
    count_x, count_y, count_z = (lax.axis_size("gx"), lax.axis_size("gy"), lax.axis_size("gz"))
    index_x, index_y, index_z = (lax.axis_index("gx"), lax.axis_index("gy"), lax.axis_index("gz"))
    one = jnp.float32(1.0)
    zero = jnp.float32(0.0)
    edges = {
        1: lower_weight(sx, jnp.where(index_x > 0, one, zero))[:, None, None],
        2: upper_weight(sx, jnp.where(index_x < count_x - 1, one, zero))[:, None, None],
        5: lower_weight(sz, jnp.where(index_z > 0, one, zero)),
        6: upper_weight(sz, jnp.where(index_z < count_z - 1, one, zero)),
    }
    first_y = index_y == 0
    last_y = index_y == count_y - 1
    far_cells = (cell_codes == 2).astype(jnp.float32)
    wall_cells = (cell_codes == 1).astype(jnp.float32)
    fields = block_basis.shape[1]
    field_one = (jnp.arange(fields) == 1).astype(jnp.float32)
    penalty = (far_cells[None] + 2.0 * wall_cells[None] * field_one[:, None, None, None])[:, None]
    padded_list = []
    for blk in range(block_basis.shape[0]):
        padded = with_halo(block_basis[blk], (("gx", 2), ("gy", 3), ("gz", 4)), 1)
        padded_list.append(padded.astype(jnp.float32))
    rotated = rotate_rims(padded_list[0], padded_list[1], cosine, sine, first_y, last_y)
    stiff_cols = []
    mass_cols = []
    for blk in range(block_basis.shape[0]):
        stiff, mass = block_terms(
            block_basis[blk], rotated[blk], resident_basis, jacobian, volumes, penalty, edges
        )
        stiff_cols.append(stiff)
        mass_cols.append(mass)
    stiff_local = jnp.concatenate(stiff_cols, axis=1)
    mass_local = jnp.concatenate(mass_cols, axis=1)
    scale = 1.0 / math.sqrt(fields * sx * sy * sz * count_x * count_y * count_z)
    stiff_sum, mass_sum = lax.psum((stiff_local, mass_local), ("gx", "gy", "gz"))
    return (stiff_sum * scale, mass_sum * scale)


def solution(mesh):
    return jax.shard_map(
        shards,
        mesh=mesh,
        in_specs=(
            P(None, None, "gx", "gy", "gz"),
            P(None, None, None, "gx", "gy", "gz"),
            P(None, None, None, "gx", "gy", "gz"),
            P("gx", "gy", "gz"),
            P("gx", "gy", "gz"),
            P(),
        ),
        out_specs=(P(), P()),
        check_vma=False,
    )
```

profile of v0, /device:TPU:1, one launch (start us, length us, event | category | flops | bytes accessed | tf_op | source)
XLA Modules:
  0.0 594.4 jit_solution(14888700031939080467)
XLA Ops:
  7.2 3.1 fusion.172
  10.3 11.5 %fusion.170 = (f32[5,32,4,8,256]{4,1,3,2,0:T(8,128)}, bf16[5,32,4,8,256]{4,1,3,2,0:T(8,128)(2,1)S(1)}, bf16[5,32,4,8,256]{4,1,3,2,0:T(8,128)(2,1)S(1)}, f32[5,32,4,8,256]{4,1,3,2,0:T(8,128)}) fusion(bf16[1,5,32,4,8,256]{5,4,3,2,1,0:T(8,128)(2,1)S(1)} %get-tuple-element.134, bf16[1,5,32,4,8,256]{5,4,3,2,1,0:T(8,128)(2,1)S(1)} %get-tuple-element.135), kind=kLoop, calls=%fused_computation.307 | loop fusion | flops 2621440 | bytes 20971520 | tf_op jit(solution)/shard_map/convert_element_type | solution.py:60
  21.9 1.2 fusion.176
  23.1 2.5 collective-permute-start.6
  25.6 2.1 collective-permute-start.7
  27.7 1.2 fusion.175
  29.0 2.9 collective-permute-start.1
  31.9 1.6 bitcast_convert_fusion.34
  33.5 1.5 bitcast_convert_fusion.33
  35.1 16.1 %fusion.164 = f32[256,32]{0,1:T(8,128)} fusion(bf16[5,256,4,8,256]{4,3,2,1,0:T(8,128)(2,1)} %param.14, f32[4,8,256]{2,1,0:T(8,128)S(1)} %copy-done.15, bf16[1,5,32,4,8,256]{5,4,3,2,1,0:T(8,128)(2,1)S(1)} %get-tuple-element.134), kind=kOutput, calls=%fused_computation.182 | convolution fusion | flops 675020800 | bytes 23658496 | tf_op jit(solution)/shard_map/dot_general | solution.py:73
  51.2 26.2 %fusion.167 = f32[256,32]{0,1:T(8,128)} fusion(bf16[5,256,4,8,256]{4,3,2,1,0:T(8,128)(2,1)} %param.14, f32[4,8,256]{2,1,0:T(8,128)S(1)} %copy-done.15, bf16[1,5,32,4,8,256]{5,4,3,2,1,0:T(8,128)(2,1)S(1)} %get-tuple-element.135), kind=kOutput, calls=%fused_computation.183 | convolution fusion | flops 675020800 | bytes 23658496 | tf_op jit(solution)/shard_map/dot_general | solution.py:73
  77.3 0.7 add_negate_fusion
  78.1 4.9 slice_bitcast_fusion.69
  83.8 0.6 pad_maximum_fusion.9
  84.5 1.1 pad_maximum_fusion.4
  85.6 1.4 collective-permute-start.8
  87.0 1.5 collective-permute-start.9
  88.5 5.1 slice_bitcast_fusion.34
  93.6 2.1 pad_maximum_fusion.7
  95.7 2.7 collective-permute-start.3
  98.4 0.8 copy-done.9
  99.1 2.2 pad_maximum_fusion.1
  101.3 3.6 fusion.174
  104.9 4.4 copy.22
  109.3 4.1 collective-permute-start.10
  113.5 4.4 copy.23
  117.9 2.7 pad_maximum_fusion
  120.6 3.6 fusion.173
  124.2 4.4 copy.17
  128.6 1.7 collective-permute-start.4
  130.4 4.4 copy.18
  134.9 3.8 copy.24
  138.7 3.8 copy.25
  142.5 12.4 %maximum_convert_fusion.1 = f32[5,32,6,10,258]{4,1,3,2,0:T(8,128)} fusion(bf16[5,32,6,10,1]{4,1,3,2,0:T(8,128)(2,1)} %copy.25, bf16[5,32,6,1,256]{4,1,3,2,0:T(8,128)(2,1)} %copy-done.10, bf16[5,32,1,8,256]{4,1,3,2,0:T(8,128)(2,1)} %collective-permute-done.7, bf16[5,32,4,8,256]{4,1,3,2,0:T(8,128)(2,1)S(1)} %get-tuple-element.191, ...), kind=kLoop, calls=%fused_computation.9 | loop fusion | flops 34675200 | bytes 14860800 | tf_op jit(solution)/shard_map/convert_element_type | solution.py:113
  154.9 12.9 %copy.79 = f32[5,32,6,10,258]{4,1,3,2,0:T(8,128)} copy(f32[5,32,6,10,258]{4,1,3,2,0:T(8,128)} %maximum_convert_fusion.1) | data formatting | bytes 19814400
  167.8 4.0 copy.19
  171.8 3.9 copy.20
  175.6 12.8 %maximum_convert_fusion = f32[5,32,6,10,258]{4,1,3,2,0:T(8,128)} fusion(bf16[5,32,6,10,1]{4,1,3,2,0:T(8,128)(2,1)} %copy.20, bf16[5,32,6,1,256]{4,1,3,2,0:T(8,128)(2,1)} %collective-permute-done.3, bf16[5,32,1,8,256]{4,1,3,2,0:T(8,128)(2,1)} %collective-permute-done.1, bf16[5,32,4,8,256]{4,1,3,2,0:T(8,128)(2,1)S(1)} %copy-done.2, ...), kind=kLoop, calls=%fused_computation.8 | loop fusion | flops 34675200 | bytes 14860800 | tf_op jit(solution)/shard_map/convert_element_type | solution.py:113
  188.4 13.0 %copy.78 = f32[5,32,6,10,258]{4,1,3,2,0:T(8,128)} copy(f32[5,32,6,10,258]{4,1,3,2,0:T(8,128)} %maximum_convert_fusion) | data formatting | bytes 19814400
  201.4 3.9 select_dynamic-update-slice_fusion.3
  205.2 3.9 select_dynamic-update-slice_fusion.2
  209.1 12.4 %slice_bitcast_fusion.54 = (f32[32,4,8,256]{3,0,2,1:T(8,128)}, f32[32,4,8,256]{3,0,2,1:T(8,128)}, f32[32,4,8,256]{3,0,2,1:T(8,128)}, f32[32,4,8,256]{3,0,2,1:T(8...) fusion(f32[5,32,6,10,258]{4,1,3,2,0:T(8,128)} %get-tuple-element.52), kind=kLoop, calls=%fused_computation.238 | loop fusion | bytes 20971520 | tf_op jit(solution)/shard_map/mul | solution.py:67
  221.5 12.2 %slice_bitcast_fusion.19 = (f32[32,4,8,256]{3,0,2,1:T(8,128)}, f32[32,4,8,256]{3,0,2,1:T(8,128)}, f32[32,4,8,256]{3,0,2,1:T(8,128)}, f32[32,4,8,256]{3,0,2,1:T(8...) fusion(f32[5,32,6,10,258]{4,1,3,2,0:T(8,128)} %get-tuple-element.53), kind=kLoop, calls=%fused_computation.203 | loop fusion | bytes 20971520 | tf_op jit(solution)/shard_map/mul | solution.py:67
  233.7 31.3 %slice_multiply_fusion.3 = (f32[5,32,4,8,256]{4,1,3,2,0:T(8,128)}, f32[5,32,4,8,256]{4,1,3,2,0:T(8,128)}, f32[5,32,4,8,256]{4,1,3,2,0:T(8,128)}, f32[5,32,4,8,25...) fusion(f32[5,32,6,10,258]{4,1,3,2,0:T(8,128)} %get-tuple-elemen, ...), kind=kLoop, calls=%fused_computation.13 | loop fusion | flops 10485760 | bytes 83888160 | tf_op jit(solution)/shard_map/mul | solution.py:64
  265.0 5.0 slice_bitcast_fusion.44
  270.1 2.7 slice_bitcast_fusion.39
  272.8 2.6 slice_bitcast_fusion.64
  275.3 0.8 slice-done.3
  276.1 2.7 slice_bitcast_fusion.59
  278.8 0.7 copy-done.6
  279.6 0.1 copy-done.12
  279.8 39.5 %multiply_convert_fusion.20 = bf16[5,32,4,8,256]{4,1,3,2,0:T(8,128)(2,1)} fusion(f32[32,4,8,256]{3,0,2,1:T(8,128)} %get-tuple-element.105, f32[5,4,8,256]{3,2,1,0:T(8,128)} %get-tuple-element.177, f32[32,4,8,256]{3,0,2,1:T(8,128)} %get-tuple-element.106, f32[5,4,8,256]{3,2,1,0:T(8,128)} %get-tuple-element.178, ...), kind=kLoop, calls=%fused_computation.21.clone.clone.clone.clone.1 | loop fusion | flops 96993280 | bytes 47874048 | tf_op jit(solution)/shard_map/dot_general | solution.py:73
  319.3 34.6 %fusion.158 = f32[256,32]{0,1:T(8,128)S(1)} fusion(bf16[5,256,4,8,256]{4,3,2,1,0:T(8,128)(2,1)} %param.14, bf16[5,32,4,8,256]{4,1,3,2,0:T(8,128)(2,1)} %multiply_convert_fusion.20), kind=kOutput, calls=%fused_computation.180 | convolution fusion | flops 671088640 | bytes 23625728 | tf_op jit(solution)/shard_map/dot_general | solution.py:73
  353.9 4.9 slice_bitcast_fusion.29
  358.9 5.0 slice_bitcast_fusion.24
  363.9 5.0 slice_bitcast_fusion.9
  369.0 2.6 slice_bitcast_fusion.4
  371.6 0.8 copy-done.4
  372.4 37.9 %multiply_convert_fusion.21 = bf16[5,32,4,8,256]{4,1,3,2,0:T(8,128)(2,1)} fusion(f32[32,4,8,256]{3,0,2,1:T(8,128)} %get-tuple-element.130, f32[32,4,8,256]{3,0,2,1:T(8,128)} %get-tuple-element.131, f32[32,4,8,256]{3,0,2,1:T(8,128)} %get-tuple-element.132, f32[32,4,8,256]{3,0,2,1:T(8,128)} %get-tuple-element.133, ...), kind=kLoop, calls=%fused_computation.20.clone.clone.clone.clone.1 | loop fusion | flops 96993280 | bytes 47874048 | tf_op jit(solution)/shard_map/dot_general | solution.py:73
  410.4 34.3 %fusion.161 = f32[256,32]{0,1:T(8,128)S(1)} fusion(bf16[5,256,4,8,256]{4,3,2,1,0:T(8,128)(2,1)} %param.14, bf16[5,32,4,8,256]{4,1,3,2,0:T(8,128)(2,1)} %multiply_convert_fusion.21), kind=kOutput, calls=%fused_computation.181 | convolution fusion | flops 671088640 | bytes 23625728 | tf_op jit(solution)/shard_map/dot_general | solution.py:73
  444.6 0.6 pad_maximum_fusion.8
  445.3 139.0 %all-reduce.3.cloned.1.call-done = (f32[256,64]{0,1:T(8,128)}, f32[256,64]{0,1:T(8,128)}) async-done(((f32[256,64]{0,1:T(8,128)}, f32[256,64]{0,1:T(8,128)}), (f32[256,64]{0,1:T(8,128)}, f32[256,64]{0,1:T(8,128)})) %all-reduce.3.cloned.1.call-update) | async-done | bytes 131088 | tf_op jit(solution)/shard_map/psum | solution.py:126
  584.3 1.5 broadcast_multiply_fusion
  585.7 1.5 broadcast_multiply_fusion.1
  (66 shorter events, 0.5 us)
Async XLA Ops:
  7.2 577.1 %all-reduce.3.cloned.1.call-start = ((), (), s32[]{:S(2)}) async-start(), calls=%async_computation | async-start | bytes 262144 | tf_op jit(solution)/shard_map/psum | solution.py:126
  10.3 24.7 %copy-start.5 = (bf16[1,5,32,4,8,256]{5,4,3,2,1,0:T(8,128)(2,1)}, bf16[1,5,32,4,8,256]{5,4,3,2,1,0:T(8,128)(2,1)S(1)}, u32[]{:S(2)}) copy-start(bf16[1,5,32,4,8,256]{5,4,3,2,1,0:T(8,128)(2,1)S(1)} %get-tuple-element.134) | copy-start | bytes 7864324
  10.3 40.8 %copy-start.3 = (bf16[1,5,32,4,8,256]{5,4,3,2,1,0:T(8,128)(2,1)}, bf16[1,5,32,4,8,256]{5,4,3,2,1,0:T(8,128)(2,1)S(1)}, u32[]{:S(2)}) copy-start(bf16[1,5,32,4,8,256]{5,4,3,2,1,0:T(8,128)(2,1)S(1)} %get-tuple-element.135) | copy-start | bytes 7864324
  21.9 13.1 %copy-start = (bf16[5,32,4,8,256]{4,1,3,2,0:T(8,128)(2,1)}, bf16[5,32,4,8,256]{4,1,3,2,0:T(8,128)(2,1)S(1)}, u32[]{:S(2)}) copy-start(bf16[5,32,4,8,256]{4,1,3,2,0:T(8,128)(2,1)S(1)} %get-tuple-element.180) | copy-start | bytes 7864324
  21.9 10.0 %copy-start.8 = (bf16[7,5,5,4,8,256]{5,4,3,2,1,0:T(8,128)(2,1)S(1)}, bf16[7,5,5,4,8,256]{5,4,3,2,1,0:T(8,128)(2,1)}, u32[]{:S(2)}) copy-start(bf16[7,5,5,4,8,256]{5,4,3,2,1,0:T(8,128)(2,1)} %param.16) | copy-start | bytes 8601604
  23.1 61.4 %collective-permute-start.6 = (bf16[5,32,1,8,256]{4,1,3,2,0:T(8,128)(2,1)}, bf16[5,32,1,8,256]{4,1,3,2,0:T(8,128)(2,1)}, u32[]{:S(2)}, u32[]{:S(2)}) collective-permute-start(bf16[5,32,1,8,256]{4,1,3,2,0:T(8,128)(2,1)} %get-tuple-element.185), channel_id=1, source_target_pairs={{0,32},{32,64},{64,96},{96,0},{1,33},{33,65},{65,97},{97,1},{2,34}... | collective-permute-start | bytes 1966088 | tf_op jit(solution)/shard_map/ppermute | solution.py:17
  25.6 58.9 %collective-permute-start.7 = (bf16[5,32,1,8,256]{4,1,3,2,0:T(8,128)(2,1)}, bf16[5,32,1,8,256]{4,1,3,2,0:T(8,128)(2,1)}, u32[]{:S(2)}, u32[]{:S(2)}) collective-permute-start(bf16[5,32,1,8,256]{4,1,3,2,0:T(8,128)(2,1)} %get-tuple-element.186), channel_id=1, source_target_pairs={{32,0},{64,32},{96,64},{0,96},{33,1},{65,33},{97,65},{1,97},{34,2}... | collective-permute-start | bytes 1966088 | tf_op jit(solution)/shard_map/ppermute | solution.py:20
  27.7 7.3 %copy-start.16 = (s32[4,8,256]{2,1,0:T(8,128)S(1)}, s32[4,8,256]{2,1,0:T(8,128)}, u32[]{:S(2)}) copy-start(s32[4,8,256]{2,1,0:T(8,128)} %param.18) | copy-start | bytes 98308
  27.7 7.4 %copy-start.15 = (f32[4,8,256]{2,1,0:T(8,128)S(1)}, f32[4,8,256]{2,1,0:T(8,128)}, u32[]{:S(2)}) copy-start(f32[4,8,256]{2,1,0:T(8,128)} %param.17) | copy-start | bytes 98308
  29.0 64.6 %collective-permute-start = (bf16[5,32,1,8,256]{4,1,3,2,0:T(8,128)(2,1)}, bf16[5,32,1,8,256]{4,1,3,2,0:T(8,128)(2,1)S(1)}, u32[]{:S(2)}, u32[]{:S(2)}) collective-permute-start(bf16[5,32,1,8,256]{4,1,3,2,0:T(8,128)(2,1)} %get-tuple-element.183), channel_id=1, source_target_pairs={{0,32},{32,64},{64,96},{96,0},{1,33},{33,65},{65,97},{97,1},{2,34}... | collective-permute-start | bytes 1966088 | tf_op jit(solution)/shard_map/ppermute | solution.py:17
  29.0 64.6 %collective-permute-start.1 = (bf16[5,32,1,8,256]{4,1,3,2,0:T(8,128)(2,1)}, bf16[5,32,1,8,256]{4,1,3,2,0:T(8,128)(2,1)}, u32[]{:S(2)}, u32[]{:S(2)}) collective-permute-start(bf16[5,32,1,8,256]{4,1,3,2,0:T(8,128)(2,1)} %get-tuple-element.184), channel_id=1, source_target_pairs={{32,0},{64,32},{96,64},{0,96},{33,1},{65,33},{97,65},{1,97},{34,2}... | collective-permute-start | bytes 1966088 | tf_op jit(solution)/shard_map/ppermute | solution.py:20
  78.1 5.7 copy-start.17
  78.1 5.7 copy-start.18
  85.6 12.7 %collective-permute-start.8 = (bf16[5,32,6,1,256]{4,1,3,2,0:T(8,128)(2,1)S(1)}, bf16[5,32,6,1,256]{4,1,3,2,0:T(8,128)(2,1)S(1)}, u32[]{:S(2)}, u32[]{:S(2)}) collective-permute-start(bf16[5,32,6,1,256]{4,1,3,2,0:T(8,128)(2,1)S(1)} %get-tuple-element.142), channel_id=1, source_target_pairs={{0,8},{8,16},{16,24},{24,0},{1,9},{9,17},{17,25},{25,1},{2,10},{10... | collective-permute-start | bytes 1474568 | tf_op jit(solution)/shard_map/ppermute | solution.py:17
  87.0 11.4 %collective-permute-start.9 = (bf16[5,32,6,1,256]{4,1,3,2,0:T(8,128)(2,1)S(1)}, bf16[5,32,6,1,256]{4,1,3,2,0:T(8,128)(2,1)S(1)}, u32[]{:S(2)}, u32[]{:S(2)}) collective-permute-start(bf16[5,32,6,1,256]{4,1,3,2,0:T(8,128)(2,1)S(1)} %get-tuple-element.143), channel_id=1, source_target_pairs={{8,0},{16,8},{24,16},{0,24},{9,1},{17,9},{25,17},{1,25},{10,2},{18... | collective-permute-start | bytes 1474568 | tf_op jit(solution)/shard_map/ppermute | solution.py:20
  88.5 5.1 copy-start.1
  95.7 22.2 %collective-permute-start.2 = (bf16[5,32,6,1,256]{4,1,3,2,0:T(8,128)(2,1)}, bf16[5,32,6,1,256]{4,1,3,2,0:T(8,128)(2,1)}, u32[]{:S(2)}, u32[]{:S(2)}) collective-permute-start(bf16[5,32,6,1,256]{4,1,3,2,0:T(8,128)(2,1)} %get-tuple-element.140), channel_id=1, source_target_pairs={{0,8},{8,16},{16,24},{24,0},{1,9},{9,17},{17,25},{25,1},{2,10},{10... | collective-permute-start | bytes 1474568 | tf_op jit(solution)/shard_map/ppermute | solution.py:17
  95.7 22.2 %collective-permute-start.3 = (bf16[5,32,6,1,256]{4,1,3,2,0:T(8,128)(2,1)}, bf16[5,32,6,1,256]{4,1,3,2,0:T(8,128)(2,1)}, u32[]{:S(2)}, u32[]{:S(2)}) collective-permute-start(bf16[5,32,6,1,256]{4,1,3,2,0:T(8,128)(2,1)} %get-tuple-element.141), channel_id=1, source_target_pairs={{8,0},{16,8},{24,16},{0,24},{9,1},{17,9},{25,17},{1,25},{10,2},{18... | collective-permute-start | bytes 1474568 | tf_op jit(solution)/shard_map/ppermute | solution.py:20
  98.4 0.8 copy-start.9
  99.1 5.8 copy-start.10
  109.3 25.6 %collective-permute-start.10 = (bf16[5,32,6,10,1]{1,2,4,3,0:T(8,128)(2,1)}, bf16[5,32,6,10,1]{1,2,4,3,0:T(8,128)(2,1)}, u32[]{:S(2)}, u32[]{:S(2)}) collective-permute-start(bf16[5,32,6,10,1]{1,2,4,3,0:T(8,128)(2,1)} %copy.22), channel_id=1, source_target_pairs={{0,1},{1,2},{2,3},{3,4},{4,5},{5,6},{6,7},{7,0},{8,9},{9,10},{10,1... | collective-permute-start | bytes 57608 | tf_op jit(solution)/shard_map/ppermute | solution.py:17
  117.9 20.8 %collective-permute-start.11 = (bf16[5,32,6,10,1]{1,2,4,3,0:T(8,128)(2,1)}, bf16[5,32,6,10,1]{1,2,4,3,0:T(8,128)(2,1)}, u32[]{:S(2)}, u32[]{:S(2)}) collective-permute-start(bf16[5,32,6,10,1]{1,2,4,3,0:T(8,128)(2,1)} %copy.23), channel_id=1, source_target_pairs={{1,0},{2,1},{3,2},{4,3},{5,4},{6,5},{7,6},{0,7},{9,8},{10,9},{11,1... | collective-permute-start | bytes 57608 | tf_op jit(solution)/shard_map/ppermute | solution.py:20
  128.6 39.1 %collective-permute-start.4 = (bf16[5,32,6,10,1]{1,2,4,3,0:T(8,128)(2,1)}, bf16[5,32,6,10,1]{1,2,4,3,0:T(8,128)(2,1)}, u32[]{:S(2)}, u32[]{:S(2)}) collective-permute-start(bf16[5,32,6,10,1]{1,2,4,3,0:T(8,128)(2,1)} %copy.17), channel_id=1, source_target_pairs={{0,1},{1,2},{2,3},{3,4},{4,5},{5,6},{6,7},{7,0},{8,9},{9,10},{10,1... | collective-permute-start | bytes 57608 | tf_op jit(solution)/shard_map/ppermute | solution.py:17
  134.8 37.0 %collective-permute-start.5 = (bf16[5,32,6,10,1]{1,2,4,3,0:T(8,128)(2,1)}, bf16[5,32,6,10,1]{1,2,4,3,0:T(8,128)(2,1)}, u32[]{:S(2)}, u32[]{:S(2)}) collective-permute-start(bf16[5,32,6,10,1]{1,2,4,3,0:T(8,128)(2,1)} %copy.18), channel_id=1, source_target_pairs={{1,0},{2,1},{3,2},{4,3},{5,4},{6,5},{7,6},{0,7},{9,8},{10,9},{11,1... | collective-permute-start | bytes 57608 | tf_op jit(solution)/shard_map/ppermute | solution.py:20
  167.8 7.8 %copy-start.2 = (bf16[5,32,4,8,256]{4,1,3,2,0:T(8,128)(2,1)S(1)}, bf16[5,32,4,8,256]{4,1,3,2,0:T(8,128)(2,1)}, u32[]{:S(2)}) copy-start(bf16[5,32,4,8,256]{4,1,3,2,0:T(8,128)(2,1)} %copy-done) | copy-start | bytes 7864324
  265.0 5.1 copy-start.7
  270.1 5.3 slice-start.2
  272.8 3.3 slice-start.3
  276.1 3.4 copy-start.6
  276.1 3.5 copy-start.11
  276.1 3.6 copy-start.12
  276.1 3.7 copy-start.13
  276.1 3.7 copy-start.14
  358.9 10.1 %slice-start = ((s8[5242880]{0:T(1024)(128)(4,1)}), s8[4194304]{0:T(1024)(128)(4,1)S(1)}, s32[]{:S(2)}) async-start(s8[5242880]{0:T(1024)(128)(4,1)} %bitcast.301), calls=%async_computation.1 | async-start | bytes 8388608
  363.9 5.1 slice-start.1
  369.0 3.5 copy-start.4
Sparse Core Ops, SparseCore 0:
  445.4 138.8 all-reduce.2
where the time goes:
time: 603 us; the launch traced here: 594 us
  other arithmetic  169 us (28%)
  local copies, waits for them, and re-layouts  140 us (23%)
  waiting for transfers between devices  139 us (23%)
  matrix products  111 us (18%)
  starting transfers between devices  19.1 us (3%)
  between operations  15.5 us (3%)
    psum x1, waiting for transfers between devices, shards(): lax.psum((stiff_local, mass_local), ('gx', 'gy', 'gz'))  139 us
    dot_general x4, matrix products, project(): lax.dot_general(resident_basis, weighted, (((0, 2, 3, 4), (0, 2, 3, 4)),...  111 us
    dot_general x2, other arithmetic, project(): lax.dot_general(resident_basis, weighted, (((0, 2, 3, 4), (0, 2, 3, 4)),...  77.4 us
    mul x12, local copies, waits for them, and re-layouts, apply_block(): jacobian[spot, :, field][:, None].astype(jnp.float32) * values[field][None]  65.2 us
    mul x1, other arithmetic, apply_block(): values = values * edges[spot]  31.3 us
    unnamed x48, local copies, waits for them, and re-layouts  29.3 us
    convert_element_type x2, other arithmetic, shards(): padded_list.append(padded.astype(jnp.float32))  25.1 us
    slice x6, local copies, waits for them, and re-layouts, with_halo(): lax.slice_in_dim(block, block.shape[dim] - width, None, axis=dim)  18.5 us
  transfers between devices with their start and end apart: 13, of which 1 were waited for; matrix products, arithmetic and copies ran while one was open for 21% of the time, Pallas kernels for 0%

commit v1 on v0

v1 whole, which is shorter than its diff:
```python
import functools
import math

import jax
import jax.numpy as jnp
from jax import lax
from jax.experimental import pallas as pl
from jax.experimental.pallas import tpu as pltpu
from jax.sharding import PartitionSpec as P

BLADES = 24
MESH = pl.DeviceIdType.MESH
NT = (((1,), (1,)), ((), ()))
F32 = jnp.float32
BF16 = jnp.bfloat16


def kernel(
    scale,
    basis_hbm,
    block_hbm,
    jac_hbm,
    vol_hbm,
    codes_hbm,
    phase_ref,
    stiff_out,
    mass_out,
    block_nat,
    jac_nat,
    vol,
    codes,
    ext,
    jac,
    basis,
    face_nat,
    face,
    rim_out,
    rim_in,
    col_out,
    col_in,
    partial,
    columns,
    total,
    gather1,
    gather2,
    gather3,
    local_sem,
    basis_sem,
    xs_sem,
    xr_sem,
    ys_sem,
    yr_sem,
    zs_sem,
    zr_sem,
    s1_sem,
    r1_sem,
    s2_sem,
    r2_sem,
    s3_sem,
    r3_sem,
):
    nb, nf, nc, nx, ny, nz = block_nat.shape
    nbc = nb * nc
    ix, iy, iz = (lax.axis_index(a) for a in ("gx", "gy", "gz"))
    cx, cy, cz = (lax.axis_size(a) for a in ("gx", "gy", "gz"))
    plane = cx * cy
    me2 = ix * cy + iy

    def in_plane(index):
        return (index // cy, index % cy, iz)

    def in_line(index):
        return (ix, iy, index)

    block_copies = [
        pltpu.make_async_copy(block_hbm.at[b], block_nat.at[b], local_sem.at[b]) for b in range(nb)
    ]
    jac_copy = pltpu.make_async_copy(jac_hbm, jac_nat, local_sem.at[nb])
    vol_copy = pltpu.make_async_copy(vol_hbm, vol, local_sem.at[nb + 1])
    codes_copy = pltpu.make_async_copy(codes_hbm, codes, local_sem.at[nb + 2])
    for copy in block_copies + [jac_copy, vol_copy, codes_copy]:
        copy.start()

    def basis_copy(x, slot):
        return pltpu.make_async_copy(
            basis_hbm.at[:, :, x], basis.at[slot], basis_sem.at[slot]
        )

    basis_order = (1, 2, 0, 3)
    basis_copy(basis_order[0], 0).start()

    barrier = pltpu.get_barrier_semaphore()
    for d in range(1, cz):
        pl.semaphore_signal(
            barrier, inc=1, device_id=in_line((iz + d) % cz), device_id_type=MESH
        )
    for d in range(1, plane):
        pl.semaphore_signal(
            barrier, inc=1, device_id=in_plane((me2 + d) % plane), device_id_type=MESH
        )
    pl.semaphore_wait(barrier, cz - 1 + plane - 1)

    def face_copy(side, b):
        source, target = ((nx - 1, (ix + 1) % cx), (0, (ix + cx - 1) % cx))[side]
        return pltpu.make_async_remote_copy(
            src_ref=block_hbm.at[b, :, :, source],
            dst_ref=face_nat.at[side, b],
            send_sem=xs_sem.at[side, b],
            recv_sem=xr_sem.at[side, b],
            device_id=(target, iy, iz),
            device_id_type=MESH,
        )

    for b in range(nb):
        for side in range(2):
            face_copy(side, b).start()

    for copy in block_copies:
        copy.wait()

    def relay(x, carry):
        def one(i, carry):
            b, f = i // nf, i % nf
            rows = jnp.swapaxes(block_nat[b, f, :, x], 0, 1)
            at = pl.ds(pl.multiple_of(b * nc, nc), nc)
            ext[x, pl.ds(1, ny), f, at] = rows.astype(F32)
            rim_out[1, x, f, at] = rows[0]
            rim_out[0, x, f, at] = rows[ny - 1]
            return carry

        return lax.fori_loop(0, nb * nf, one, carry)

    def rim_copy(side):
        target = ((iy + 1) % cy, (iy + cy - 1) % cy)[side]
        return pltpu.make_async_remote_copy(
            src_ref=rim_out.at[side],
            dst_ref=rim_in.at[side],
            send_sem=ys_sem.at[side],
            recv_sem=yr_sem.at[side],
            device_id=(ix, target, iz),
            device_id_type=MESH,
        )

    lax.fori_loop(0, nx, relay, 0)
    for side in range(2):
        rim_copy(side).start()

    lane = lax.broadcasted_iota(jnp.int32, (nf, nbc, 128), 2)
    col_out[...] = jnp.zeros_like(col_out)

    def pack(j, carry):
        x, y = j // ny, j % ny
        here = lane == j
        for f in range(nf):
            last = pltpu.roll(ext[x, 1 + y, f, :, nz - 128 :], j + 1, 1)
            first = pltpu.roll(ext[x, 1 + y, f, :, :128], j, 1)
            col_out[0, f] = jnp.where(here[f], last, col_out[0, f])
            col_out[1, f] = jnp.where(here[f], first, col_out[1, f])
        return carry

    lax.fori_loop(0, nx * ny, pack, 0)

    def col_copy(side):
        target = ((iz + 1) % cz, (iz + cz - 1) % cz)[side]
        return pltpu.make_async_remote_copy(
            src_ref=col_out.at[side],
            dst_ref=col_in.at[side],
            send_sem=zs_sem.at[side],
            recv_sem=zr_sem.at[side],
            device_id=in_line(target),
            device_id_type=MESH,
        )

    for side in range(2):
        col_copy(side).start()

    for copy in (jac_copy, vol_copy, codes_copy):
        copy.wait()

    count = 7 * nf * nf

    def blocks(x, carry):
        volume = vol[x]
        code = codes[x]
        far = jnp.where(code == 2, 1.0, 0.0).astype(F32)
        wall = jnp.where(code == 1, 2.0, 0.0).astype(F32)
        for first in range(0, count + 1, 8):
            group = []
            for k in range(first, first + 8):
                s, f, g = k // (nf * nf), (k // nf) % nf, k % nf
                if k == count:
                    value = volume
                else:
                    value = jac_nat[s, g, f, x].astype(F32)
                    if s == 0 and g == f:
                        value = value - (far + wall if g == 1 else far)
                    value = value * volume
                group.append(value)
            jac[x, :, pl.ds(first, 8)] = jnp.swapaxes(jnp.stack(group), 0, 1)
        return carry

    lax.fori_loop(0, nx, blocks, 0)

    for side in range(2):
        col_copy(side).wait()
    col_in[0] = col_in[0] * jnp.where(iz > 0, 1.0, 0.0).astype(F32)
    col_in[1] = col_in[1] * jnp.where(iz < cz - 1, 1.0, 0.0).astype(F32)

    lane2 = lax.broadcasted_iota(jnp.int32, (nc, 128), 1)
    halves = nz // 128

    def stencil(x, y, b, sides):
        at = pl.ds(pl.multiple_of(b * nc, nc), nc)
        j = x * ny + y
        for half in range(halves):
            lanes = pl.ds(half * 128, 128)
            acc = [None] * nf

            def add(s, f, values):
                for g in range(nf):
                    term = jac[x, y, pl.ds((s * nf + f) * nf + g, 1), lanes] * values
                    acc[g] = term if acc[g] is None else acc[g] + term

            for f in range(nf):
                here = ext[x, 1 + y, f, at, lanes]
                add(0, f, here)
                for s, xn in sides:
                    add(s, f, ext[xn, 1 + y, f, at, lanes])
                add(3, f, ext[x, y, f, at, lanes])
                add(4, f, ext[x, 2 + y, f, at, lanes])
                if half == 0:
                    before = pltpu.roll(col_in[0, f, at], (128 - j) % 128, 1)
                else:
                    before = pltpu.roll(ext[x, 1 + y, f, at, pl.ds(half * 128 - 128, 128)], 1, 1)
                add(5, f, jnp.where(lane2 == 0, before, pltpu.roll(here, 1, 1)))
                if half == halves - 1:
                    after = pltpu.roll(col_in[1, f, at], 127 - j, 1)
                else:
                    after = pltpu.roll(ext[x, 1 + y, f, at, pl.ds(half * 128 + 128, 128)], 127, 1)
                add(6, f, jnp.where(lane2 == 127, after, pltpu.roll(here, 127, 1)))
                mass = (here * jac[x, y, pl.ds(count, 1), lanes]).astype(BF16)
                columns[x, f, y, pl.ds(pl.multiple_of(nbc + b * nc, nc), nc), lanes] = mass
            yield half, lanes, acc

    def inner_row(x, y, b):
        at = pl.ds(pl.multiple_of(b * nc, nc), nc)
        for _, lanes, acc in stencil(x, y, b, ((1, x - 1), (2, x + 1))):
            for g in range(nf):
                columns[x, g, y, at, lanes] = acc[g].astype(BF16)

    def outer_row(k, y, b):
        at = pl.ds(pl.multiple_of(b * nc, nc), nc)
        x = k * (nx - 1)
        for _, lanes, acc in stencil(x, y, b, ((2 - k, 1 + k * (nx - 3)),)):
            for g in range(nf):
                partial[k, y, g, at, lanes] = acc[g]

    def rows(low, count, stride):
        def inner(i, carry):
            inner_row(1 + i // (count * nb), low + stride * ((i // nb) % count), i % nb)
            return carry

        lax.fori_loop(0, (nx - 2) * count * nb, inner, 0)
        for k in range(2):

            def outer(i, carry, k=k):
                outer_row(k, low + stride * (i // nb), i % nb)
                return carry

            lax.fori_loop(0, count * nb, outer, 0)

    rows(1, ny - 2, 1)

    phase = jnp.full((8, 128), phase_ref[0], jnp.int32).astype(F32)
    sigma = 2.0 * math.pi * phase / BLADES
    cosine = jnp.cos(sigma)[:1, :1]
    sine = jnp.sin(sigma)[:1, :1]
    for side in range(2):
        rim_copy(side).wait()
        at_end = (iy == 0, iy == cy - 1)[side]
        turn_c = jnp.where(at_end, cosine, 1.0)
        turn_s = jnp.where(at_end, sine if side == 0 else -sine, 0.0)
        row = 0 if side == 0 else ny + 1

        def turn(i, carry, side=side, row=row, turn_c=turn_c, turn_s=turn_s):
            x, f = i // nf, i % nf
            re = rim_in[side, x, f, :nc].astype(F32)
            im = rim_in[side, x, f, nc:].astype(F32)
            ext[x, row, f, :nc] = turn_c * re + turn_s * im
            ext[x, row, f, nc:] = turn_c * im - turn_s * re
            return carry

        lax.fori_loop(0, nx * nf, turn, 0)

    rows(0, 2, ny - 1)

    total[...] = jnp.zeros_like(total)

    def project(x, slot):
        def one(g, carry):
            left = jnp.swapaxes(basis[slot, g], 0, 1)
            left = jnp.concatenate([left[y] for y in range(ny)], axis=1)
            right = jnp.concatenate([columns[x, g, y] for y in range(ny)], axis=1)
            total[...] += lax.dot_general(left, right, NT, preferred_element_type=F32)
            return carry

        lax.fori_loop(0, nf, one, 0)

    basis_copy(basis_order[1], 1).start()
    for i in range(2):
        basis_copy(basis_order[i], i).wait()
        project(basis_order[i], i)
        basis_copy(basis_order[i + 2], i).start()

    keep = (jnp.where(ix > 0, 1.0, 0.0).astype(F32), jnp.where(ix < cx - 1, 1.0, 0.0).astype(F32))
    for b in range(nb):
        for side in range(2):
            face_copy(side, b).wait()
            for f in range(nf):
                face[side, :, f] = jnp.swapaxes(face_nat[side, b, f], 0, 1).astype(F32) * keep[side]

            def finish(y, carry, side=side, b=b):
                x = side * (nx - 1)
                at = pl.ds(b * nc, nc)
                for half in range(halves):
                    lanes = pl.ds(half * 128, 128)
                    acc = [partial[side, y, g, at, lanes] for g in range(nf)]
                    for f in range(nf):
                        values = face[side, y, f, :, lanes]
                        for g in range(nf):
                            acc[g] = acc[g] + jac[x, y, pl.ds(((1 + side) * nf + f) * nf + g, 1), lanes] * values
                    for g in range(nf):
                        columns[x, g, y, at, lanes] = acc[g].astype(BF16)
                return carry

            lax.fori_loop(0, ny, finish, 0)
    for i in range(2):
        basis_copy(basis_order[i + 2], i).wait()
        project(basis_order[i + 2], i)

    chunk = total.shape[0] // cz

    def copy1(d):
        target = (iz + d) % cz
        return pltpu.make_async_remote_copy(
            src_ref=total.at[pl.ds(pl.multiple_of(target * chunk, chunk), chunk)],
            dst_ref=gather1.at[d],
            send_sem=s1_sem.at[d],
            recv_sem=r1_sem.at[d],
            device_id=in_line(target),
            device_id_type=MESH,
        )

    for d in range(1, cz):
        copy1(d).start()
    own = total[pl.ds(pl.multiple_of(iz * chunk, chunk), chunk)]
    for d in range(1, cz):
        copy1(d).wait()
        own = own + gather1[d]
    gather2[me2] = own

    def copy2(d):
        return pltpu.make_async_remote_copy(
            src_ref=gather2.at[me2],
            dst_ref=gather2.at[me2],
            send_sem=s2_sem.at[d],
            recv_sem=r2_sem.at[d],
            device_id=in_plane((me2 + d) % plane),
            device_id_type=MESH,
        )

    for d in range(1, plane):
        copy2(d).start()
    for d in range(1, plane):
        copy2(d).wait()
    own = gather2[0]
    for i in range(1, plane):
        own = own + gather2[i]
    gather3[iz] = own * scale

    def copy3(d):
        return pltpu.make_async_remote_copy(
            src_ref=gather3.at[iz],
            dst_ref=gather3.at[iz],
            send_sem=s3_sem.at[d],
            recv_sem=r3_sem.at[d],
            device_id=in_line((iz + d) % cz),
            device_id_type=MESH,
        )

    for d in range(1, cz):
        copy3(d).start()
    for d in range(1, cz):
        copy3(d).wait()
    for i in range(cz):
        stiff_out[pl.ds(i * chunk, chunk)] = gather3[i, :, :nbc]
        mass_out[pl.ds(i * chunk, chunk)] = gather3[i, :, nbc:]


def shards(resident_basis, block_basis, jacobian, volumes, cell_codes, phase_index):
    nf, nr, nx, ny, nz = resident_basis.shape
    nb, _, nc = block_basis.shape[:3]
    nbc = nb * nc
    cx, cy, cz = (lax.axis_size(a) for a in ("gx", "gy", "gz"))
    scale = 1.0 / math.sqrt(nf * nx * ny * nz * cx * cy * cz)
    dma = pltpu.SemaphoreType.DMA
    anywhere = pl.BlockSpec(memory_space=pl.ANY)
    vmem = pl.BlockSpec(memory_space=pltpu.VMEM)
    out = jax.ShapeDtypeStruct((nr, nbc), F32)
    return pl.pallas_call(
        functools.partial(kernel, scale),
        out_shape=(out, out),
        in_specs=[anywhere] * 5 + [pl.BlockSpec(memory_space=pltpu.SMEM)],
        out_specs=(vmem, vmem),
        scratch_shapes=[
            pltpu.VMEM(block_basis.shape, BF16),
            pltpu.VMEM(jacobian.shape, BF16),
            pltpu.VMEM(volumes.shape, F32),
            pltpu.VMEM(cell_codes.shape, jnp.int32),
            pltpu.VMEM((nx, ny + 2, nf, nbc, nz), F32),
            pltpu.VMEM((nx, ny, 7 * nf * nf + 1, nz), F32),
            pltpu.VMEM((2, nf, nr, ny, nz), BF16),
            pltpu.VMEM((2, nb, nf, nc, ny, nz), BF16),
            pltpu.VMEM((2, ny, nf, nc, nz), F32),
            pltpu.VMEM((2, nx, nf, nbc, nz), BF16),
            pltpu.VMEM((2, nx, nf, nbc, nz), BF16),
            pltpu.VMEM((2, nf, nbc, 128), F32),
            pltpu.VMEM((2, nf, nbc, 128), F32),
            pltpu.VMEM((2, ny, nf, nbc, nz), F32),
            pltpu.VMEM((nx, nf, ny, 2 * nbc, nz), BF16),
            pltpu.VMEM((nr, 2 * nbc), F32),
            pltpu.VMEM((cz, nr // cz, 2 * nbc), F32),
            pltpu.VMEM((cx * cy, nr // cz, 2 * nbc), F32),
            pltpu.VMEM((cz, nr // cz, 2 * nbc), F32),
            dma((nb + 3,)),
            dma((2,)),
            dma((2, nb)),
            dma((2, nb)),
            dma((2,)),
            dma((2,)),
            dma((2,)),
            dma((2,)),
            dma((cz,)),
            dma((cz,)),
            dma((cx * cy,)),
            dma((cx * cy,)),
            dma((cz,)),
            dma((cz,)),
        ],
        compiler_params=pltpu.CompilerParams(
            collective_id=0, has_side_effects=True, vmem_limit_bytes=63 * 2**20
        ),
        name="galerkin",
    )(resident_basis, block_basis, jacobian, volumes, cell_codes, phase_index)


def solution(mesh):
    return jax.shard_map(
        shards,
        mesh=mesh,
        in_specs=(
            P(None, None, "gx", "gy", "gz"),
            P(None, None, None, "gx", "gy", "gz"),
            P(None, None, None, "gx", "gy", "gz"),
            P("gx", "gy", "gz"),
            P("gx", "gy", "gz"),
            P(),
        ),
        out_specs=(P(), P()),
        check_vma=False,
    )
```

time: 603 us -> 81.3 us (0.13); the launches traced: 594 us -> 81.2 us
  other arithmetic: 169 us -> 0 us
  waiting for transfers between devices: 139 us -> 0 us
  local copies, waits for them, and re-layouts: 140 us -> 3.23 us
  matrix products: 111 us -> 0 us
  Pallas kernels: 0 us -> 76.6 us
  starting transfers between devices: 19.1 us -> 0 us
  between operations: 15.5 us -> 1.29 us
    psum x1 -> x0, waiting for transfers between devices: 139 us -> none  [shards(): lax.psum((stiff_local, mass_local), ('gx', 'gy', 'gz'))]
    dot_general x4 -> x0, matrix products: 111 us -> none  [project(): lax.dot_general(resident_basis, weighted, (((0, 2, 3, 4), (0, 2, 3, 4)),...]
    dot_general x2 -> x0, other arithmetic: 77.4 us -> none  [project(): lax.dot_general(resident_basis, weighted, (((0, 2, 3, 4), (0, 2, 3, 4)),...]
    pallas_call x0 -> x1, Pallas kernels: none -> 76.6 us  [shards(): pl.pallas_call(functools.partial(kernel, scale), out_shape=(out, out), in...]
    mul x12 -> x0, local copies, waits for them, and re-layouts: 65.2 us -> none  [apply_block(): jacobian[spot, :, field][:, None].astype(jnp.float32) * values[field][None]]
    convert_element_type x7 -> x0, other arithmetic: 39.8 us -> none  [the longest x2 25.1 us: shards(): padded_list.append(padded.astype(jnp.float32))]
    mul x4 -> x0, other arithmetic: 34.3 us -> none  [the longest x1 31.3 us: apply_block(): values = values * edges[spot]]
    slice x9 -> x0, local copies, waits for them, and re-layouts: 30.4 us -> none  [the longest x6 18.5 us: with_halo(): lax.slice_in_dim(block, block.shape[dim] - width, None, axis=dim)]
  transfers between devices with their start and end apart: 13 -> 0, of which waited for: 1 -> 0; matrix products, arithmetic and copies ran while one was open for 21% -> 0% of each run, Pallas kernels for 0% -> 0%
where the time goes in v1:
time: 81.3 us; the launch traced here: 81.2 us
  Pallas kernels  76.6 us (94%)
  local copies, waits for them, and re-layouts  3.23 us (4%)
  between operations  1.29 us (2%)
    pallas_call x1, Pallas kernels, shards(): pl.pallas_call(functools.partial(kernel, scale), out_shape=(out, out), in...  76.6 us
    pallas_call x2, local copies, waits for them, and re-layouts, shards(): pl.pallas_call(functools.partial(kernel, scale), out_shape=(out, out), in...  3.23 us

profile of v1, /device:TPU:1, one launch (start us, length us, event | category | flops | bytes accessed | tf_op | source)
XLA Modules:
  0.0 81.2 jit_solution(11005392185183349230)
XLA Ops:
  1.3 76.6 %galerkin.1 = (f32[256,64]{1,0:T(8,128)}, f32[256,64]{1,0:T(8,128)}) custom-call(bf16[5,256,4,8,256]{4,3,2,1,0:T(8,128)(2,1)} %basis_hbm.1, bf16[2,5,32,4,8,256]{5,4,3,2,1,0:T(8,128)(2,1)} %block_hbm.1, bf16[7,5,5,4,8,256]{5,4,3,2,1,0:T(8,128)(2,1)} %jac_hbm.1, f32[4,8,256]{2,1,0:T(8,128)} %vol_hbm.1, s32[4,8,256]{2,1,0:T(8,128)} %codes_hbm.1, ...), custom_call_target="tpu_custom_call" | custom-call | tf_op jit(solution)/shard_map/galerkin/pallas_call | solution.py:410
  77.9 1.6 %copy.8 = f32[256,64]{0,1:T(8,128)} copy(f32[256,64]{1,0:T(8,128)} %get-tuple-element.2) | data formatting | bytes 131072 | tf_op jit(solution)/shard_map/galerkin/pallas_call | solution.py:410
  79.6 1.6 %copy.9 = f32[256,64]{0,1:T(8,128)} copy(f32[256,64]{1,0:T(8,128)} %get-tuple-element.3) | data formatting | bytes 131072 | tf_op jit(solution)/shard_map/galerkin/pallas_call | solution.py:410

commit v2 on v1

v2 whole, which is shorter than its diff:
```python
import math

import jax
import jax.numpy as jnp
from jax import lax
from jax.experimental import pallas as pl
from jax.experimental.pallas import tpu as pltpu
from jax.sharding import PartitionSpec as P

BLADES = 24
MESH = pl.DeviceIdType.MESH
NT = (((1,), (1,)), ((), ()))
F32 = jnp.float32
BF16 = jnp.bfloat16


def kernel(
    basis_hbm,
    block_hbm,
    jac_hbm,
    vol_hbm,
    codes_hbm,
    phase_ref,
    sums_out,
    block_nat,
    jac_nat,
    vol,
    codes,
    ext,
    jac,
    basis_nat,
    swapped_a,
    swapped_b,
    face_nat,
    face,
    rim_out,
    rim_in,
    col_out,
    col_in,
    col,
    partial,
    done_a,
    done_b,
    total,
    sums,
    gather1,
    gather2,
    gather3,
    local_sem,
    basis_sem,
    xs_sem,
    xr_sem,
    ys_sem,
    yr_sem,
    zs_sem,
    zr_sem,
    s1_sem,
    r1_sem,
    s2_sem,
    r2_sem,
    s3_sem,
    r3_sem,
):
    nb, nf, nc, nx, ny, nz = block_nat.shape
    nbc = nb * nc
    ix, iy, iz = (lax.axis_index(a) for a in ("gx", "gy", "gz"))
    cx, cy, cz = (lax.axis_size(a) for a in ("gx", "gy", "gz"))
    plane = cx * cy
    me2 = ix * cy + iy

    def in_plane(index):
        return (index // cy, index % cy, iz)

    def in_line(index):
        return (ix, iy, index)

    block_copies = [
        pltpu.make_async_copy(block_hbm.at[b], block_nat.at[b], local_sem.at[b]) for b in range(nb)
    ]
    jac_copy = pltpu.make_async_copy(jac_hbm, jac_nat, local_sem.at[nb])
    vol_copy = pltpu.make_async_copy(vol_hbm, vol, local_sem.at[nb + 1])
    codes_copy = pltpu.make_async_copy(codes_hbm, codes, local_sem.at[nb + 2])
    for copy in block_copies + [jac_copy, vol_copy, codes_copy]:
        copy.start()

    order = (1, 2, 0, 3)
    piece = basis_nat.shape[1] // ny

    def basis_copy(x, i):
        at = pl.ds(pl.multiple_of(i * piece, piece), piece)
        return pltpu.make_async_copy(basis_hbm.at[:, at, x], basis_nat.at[:, at], basis_sem.at[i])

    barrier = pltpu.get_barrier_semaphore()
    for d in range(1, cz):
        pl.semaphore_signal(
            barrier, inc=1, device_id=in_line((iz + d) % cz), device_id_type=MESH
        )
    for d in range(1, plane):
        pl.semaphore_signal(
            barrier, inc=1, device_id=in_plane((me2 + d) % plane), device_id_type=MESH
        )

    def face_copy(side, b):
        source, target = ((nx - 1, (ix + 1) % cx), (0, (ix + cx - 1) % cx))[side]
        return pltpu.make_async_remote_copy(
            src_ref=block_hbm.at[b, :, :, source],
            dst_ref=face_nat.at[side, b],
            send_sem=xs_sem.at[side, b],
            recv_sem=xr_sem.at[side, b],
            device_id=(target, iy, iz),
            device_id_type=MESH,
        )

    lane = lax.broadcasted_iota(jnp.int32, (nc, 128), 1)

    def relay(i, carry):
        b, f = i // nf, i % nf
        at = pl.ds(pl.multiple_of(b * nc, nc), nc)
        last = jnp.zeros((nc, 128), F32)
        first = jnp.zeros((nc, 128), F32)
        for x in range(nx):
            rows = jnp.swapaxes(block_nat[b, f, :, x], 0, 1)
            wide = rows.astype(F32)
            ext[x, pl.ds(1, ny), f, at] = wide
            rim_out[1, x, f, at] = rows[0]
            rim_out[0, x, f, at] = rows[ny - 1]
            for y in range(ny):
                j = x * ny + y
                last = jnp.where(lane == j, pltpu.roll(wide[y, :, nz - 128 :], (j + 1) % 128, 1), last)
                first = jnp.where(lane == j, pltpu.roll(wide[y, :, :128], j, 1), first)
        col_out[0, f, at] = last.astype(BF16)
        col_out[1, f, at] = first.astype(BF16)
        return carry

    def first_basis(i, carry):
        basis_copy(order[0], i).start()
        return carry

    for b in range(nb):
        if b == nb - 1:
            pl.semaphore_wait(barrier, cz - 1 + plane - 1)
            for part in range(nb):
                for side in range(2):
                    face_copy(side, part).start()
        block_copies[b].wait()
        if b == nb - 1:
            lax.fori_loop(0, ny, first_basis, 0)
        lax.fori_loop(b * nf, (b + 1) * nf, relay, 0)

    def col_copy(side):
        target = ((iz + 1) % cz, (iz + cz - 1) % cz)[side]
        return pltpu.make_async_remote_copy(
            src_ref=col_out.at[side],
            dst_ref=col_in.at[side],
            send_sem=zs_sem.at[side],
            recv_sem=zr_sem.at[side],
            device_id=in_line(target),
            device_id_type=MESH,
        )

    def rim_copy(side, x):
        target = ((iy + 1) % cy, (iy + cy - 1) % cy)[side]
        return pltpu.make_async_remote_copy(
            src_ref=rim_out.at[side, x],
            dst_ref=rim_in.at[side, x],
            send_sem=ys_sem.at[side, x],
            recv_sem=yr_sem.at[side, x],
            device_id=(ix, target, iz),
            device_id_type=MESH,
        )

    for side in range(2):
        col_copy(side).start()
    for x in order:
        for side in range(2):
            rim_copy(side, x).start()

    for copy in (jac_copy, vol_copy, codes_copy):
        copy.wait()
    count = 7 * nf * nf

    def blocks(x, carry):
        volume = vol[x]
        code = codes[x]
        far = jnp.where(code == 2, 1.0, 0.0).astype(F32)
        wall = jnp.where(code == 1, 2.0, 0.0).astype(F32)
        for start in range(0, count + 1, 8):
            group = []
            for k in range(start, start + 8):
                s, f, g = k // (nf * nf), (k // nf) % nf, k % nf
                if k == count:
                    value = volume
                else:
                    value = jac_nat[s, g, f, x].astype(F32)
                    if s == 0 and g == f:
                        value = value - (far + wall if g == 1 else far)
                    value = value * volume
                group.append(value)
            jac[x, :, pl.ds(start, 8)] = jnp.swapaxes(jnp.stack(group), 0, 1)
        return carry

    lax.fori_loop(0, nx, blocks, 0)

    phase = jnp.full((8, 128), phase_ref[0], jnp.int32).astype(F32)
    sigma = 2.0 * math.pi * phase / BLADES
    cosine = jnp.cos(sigma)[:1, :1]
    sine = jnp.sin(sigma)[:1, :1]
    turn_c = (jnp.where(iy == 0, cosine, 1.0), jnp.where(iy == cy - 1, cosine, 1.0))
    turn_s = (jnp.where(iy == 0, sine, 0.0), jnp.where(iy == cy - 1, -sine, 0.0))
    keep_z = (jnp.where(iz > 0, 1.0, 0.0).astype(F32), jnp.where(iz < cz - 1, 1.0, 0.0).astype(F32))
    keep_x = (jnp.where(ix > 0, 1.0, 0.0).astype(F32), jnp.where(ix < cx - 1, 1.0, 0.0).astype(F32))

    def swap(n, i):
        at = pl.ds(pl.multiple_of(i * piece, piece), piece)
        basis_copy(order[n], i).wait()
        for g in range(nf):
            (swapped_a, swapped_b)[n % 2][g, :, at] = jnp.swapaxes(basis_nat[g, at], 0, 1)
        if n < nx - 1:
            basis_copy(order[n + 1], i).start()

    for n in range(2):

        def early(i, carry, n=n):
            swap(n, i)
            return carry

        lax.fori_loop(0, ny, early, 0)

    for side in range(2):
        col_copy(side).wait()
        col[side] = col_in[side].astype(F32) * keep_z[side]

    halves = nz // 128

    def stencil(x, y, b, side, done, store):
        at = pl.ds(b * nc, nc)
        j = x * ny + y
        for half in range(halves):
            lanes = pl.ds(half * 128, 128)
            acc = [None] * nf

            def add(s, f, values):
                for g in range(nf):
                    term = jac[x, y, pl.ds((s * nf + f) * nf + g, 1), lanes] * values
                    acc[g] = term if acc[g] is None else acc[g] + term

            for f in range(nf):
                here = ext[x, 1 + y, f, at, lanes]
                add(0, f, here)
                for s, xn in ((1, x - 1), (2, x + 1)):
                    if 0 <= xn < nx:
                        add(s, f, ext[xn, 1 + y, f, at, lanes])
                    elif side == 1 or b == 0:
                        add(s, f, face[b if side else 0, y, f, :, lanes])
                add(3, f, ext[x, y, f, at, lanes])
                add(4, f, ext[x, 2 + y, f, at, lanes])
                if half == 0:
                    before = pltpu.roll(col[0, f, at], (128 - j) % 128, 1)
                else:
                    before = pltpu.roll(ext[x, 1 + y, f, at, pl.ds(half * 128 - 128, 128)], 1, 1)
                add(5, f, jnp.where(lane == 0, before, pltpu.roll(here, 1, 1)))
                if half == halves - 1:
                    after = pltpu.roll(col[1, f, at], 127 - j, 1)
                else:
                    after = pltpu.roll(ext[x, 1 + y, f, at, pl.ds(half * 128 + 128, 128)], 127, 1)
                add(6, f, jnp.where(lane == 127, after, pltpu.roll(here, 127, 1)))
                mass = (here * jac[x, y, pl.ds(count, 1), lanes]).astype(BF16)
                done[f, y, pl.ds(nbc + b * nc, nc), lanes] = mass
            for g in range(nf):
                store(b, g, lanes, acc[g])

    total[...] = jnp.zeros_like(total)
    for done in (done_a, done_b):
        for g in range(nf):
            done[g, ny] = jnp.zeros(done.shape[2:], BF16)

    def project(y, swapped, done, row):
        left = jnp.concatenate([swapped[g, y] for g in range(nf)], axis=1)
        right = jnp.concatenate([done[g, row] for g in range(nf)], axis=1)
        total[...] += lax.dot_general(left, right, NT, preferred_element_type=F32)

    def load_face(side, b, slot):
        face_copy(side, b).wait()

        def one(f, carry):
            rows = jnp.swapaxes(face_nat[side, b, f], 0, 1).astype(F32)
            face[slot, :, f] = rows * keep_x[side]
            return carry

        lax.fori_loop(0, nf, one, 0)

    def finish(y):
        for half in range(halves):
            lanes = pl.ds(half * 128, 128)
            acc = [partial[y, g, :, lanes] for g in range(nf)]
            for f in range(nf):
                values = face[2, y, f, :, lanes]
                for g in range(nf):
                    acc[g] = acc[g] + jac[0, y, pl.ds((nf + f) * nf + g, 1), lanes] * values
            for g in range(nf):
                done_a[g, y, pl.ds(nc, nc), lanes] = acc[g].astype(BF16)

    swaps = (swapped_a, swapped_b)
    dones = (done_a, done_b)
    for n, x in enumerate(order):
        done = dones[n % 2]
        side = 0 if x == 0 else 1 if x == nx - 1 else None
        if n == 2:
            load_face(0, 0, 0)
        if n == 3:

            def late(i, carry):
                swap(3, i)
                return carry

            lax.fori_loop(0, ny, late, 0)
            load_face(1, 0, 0)
            load_face(0, 1, 2)
            load_face(1, 1, 1)

        def row(i, carry, n=n, x=x, side=side, done=done):
            y = (i + 1) % ny

            @pl.when(i == ny - 2)
            def _():
                for t in range(2):
                    rim_copy(t, x).wait()

                    def turn(f, carry, t=t):
                        re = rim_in[t, x, f, :nc].astype(F32)
                        im = rim_in[t, x, f, nc:].astype(F32)
                        ext[x, t * (ny + 1), f, :nc] = turn_c[t] * re + turn_s[t] * im
                        ext[x, t * (ny + 1), f, nc:] = turn_c[t] * im - turn_s[t] * re
                        return carry

                    lax.fori_loop(0, nf, turn, 0)

            def store(b, g, lanes, value):
                if side == 0 and b == 1:
                    partial[y, g, :, lanes] = value
                else:
                    done[g, y, pl.ds(b * nc, nc), lanes] = value.astype(BF16)

            if n == 2:
                swap(n, i)
            if n == 1 or n == 2:
                project(i, swaps[1 - n % 2], dones[1 - n % 2], i)
            if n == 3:
                project((y + ny - 1) % ny, swapped_a, done_a, jnp.where(i == 0, ny, (y + ny - 1) % ny))
                project((y + ny - 1) % ny, swapped_b, done_b, jnp.where(i == 0, ny, (y + ny - 1) % ny))
                finish(y)
            for b in range(nb):
                stencil(x, y, b, side, done, store)
            return carry

        lax.fori_loop(0, ny, row, 0)

    project(0, swapped_a, done_a, 0)
    project(0, swapped_b, done_b, 0)

    sums[...] = total[...].T
    chunk = sums.shape[0] // cz

    def copy1(d):
        target = (iz + d) % cz
        return pltpu.make_async_remote_copy(
            src_ref=sums.at[pl.ds(pl.multiple_of(target * chunk, chunk), chunk)],
            dst_ref=gather1.at[d],
            send_sem=s1_sem.at[d],
            recv_sem=r1_sem.at[d],
            device_id=in_line(target),
            device_id_type=MESH,
        )

    for d in range(1, cz):
        copy1(d).start()
    own = sums[pl.ds(pl.multiple_of(iz * chunk, chunk), chunk)]
    for d in range(1, cz):
        copy1(d).wait()
        own = own + gather1[d]
    gather2[me2] = own

    def copy2(d):
        return pltpu.make_async_remote_copy(
            src_ref=gather2.at[me2],
            dst_ref=gather2.at[me2],
            send_sem=s2_sem.at[d],
            recv_sem=r2_sem.at[d],
            device_id=in_plane((me2 + d) % plane),
            device_id_type=MESH,
        )

    for d in range(1, plane):
        copy2(d).start()
    for d in range(1, plane):
        copy2(d).wait()
    own = gather2[0]
    for i in range(1, plane):
        own = own + gather2[i]
    gather3[iz] = own

    def copy3(d):
        return pltpu.make_async_remote_copy(
            src_ref=gather3.at[iz],
            dst_ref=gather3.at[iz],
            send_sem=s3_sem.at[d],
            recv_sem=r3_sem.at[d],
            device_id=in_line((iz + d) % cz),
            device_id_type=MESH,
        )

    for d in range(1, cz):
        copy3(d).start()
    for d in range(1, cz):
        copy3(d).wait()
    for i in range(cz):
        sums_out[pl.ds(i * chunk, chunk)] = gather3[i]


def shards(resident_basis, block_basis, jacobian, volumes, cell_codes, phase_index):
    nf, nr, nx, ny, nz = resident_basis.shape
    nb, _, nc = block_basis.shape[:3]
    nbc = nb * nc
    cx, cy, cz = (lax.axis_size(a) for a in ("gx", "gy", "gz"))
    scale = 1.0 / math.sqrt(nf * nx * ny * nz * cx * cy * cz)
    dma = pltpu.SemaphoreType.DMA
    anywhere = pl.BlockSpec(memory_space=pl.ANY)
    sums = pl.pallas_call(
        kernel,
        out_shape=jax.ShapeDtypeStruct((2 * nbc, nr), F32),
        in_specs=[anywhere] * 5 + [pl.BlockSpec(memory_space=pltpu.SMEM)],
        out_specs=pl.BlockSpec(memory_space=pltpu.VMEM),
        scratch_shapes=[
            pltpu.VMEM(block_basis.shape, BF16),
            pltpu.VMEM(jacobian.shape, BF16),
            pltpu.VMEM(volumes.shape, F32),
            pltpu.VMEM(cell_codes.shape, jnp.int32),
            pltpu.VMEM((nx, ny + 2, nf, nbc, nz), F32),
            pltpu.VMEM((nx, ny, 7 * nf * nf + 1, nz), F32),
            pltpu.VMEM((nf, nr, ny, nz), BF16),
            pltpu.VMEM((nf, ny, nr, nz), BF16),
            pltpu.VMEM((nf, ny, nr, nz), BF16),
            pltpu.VMEM((2, nb, nf, nc, ny, nz), BF16),
            pltpu.VMEM((3, ny, nf, nc, nz), F32),
            pltpu.VMEM((2, nx, nf, nbc, nz), BF16),
            pltpu.VMEM((2, nx, nf, nbc, nz), BF16),
            pltpu.VMEM((2, nf, nbc, 128), BF16),
            pltpu.VMEM((2, nf, nbc, 128), BF16),
            pltpu.VMEM((2, nf, nbc, 128), F32),
            pltpu.VMEM((ny, nf, nc, nz), F32),
            pltpu.VMEM((nf, ny + 1, 2 * nbc, nz), BF16),
            pltpu.VMEM((nf, ny + 1, 2 * nbc, nz), BF16),
            pltpu.VMEM((nr, 2 * nbc), F32),
            pltpu.VMEM((2 * nbc, nr), F32),
            pltpu.VMEM((cz, 2 * nbc // cz, nr), F32),
            pltpu.VMEM((cx * cy, 2 * nbc // cz, nr), F32),
            pltpu.VMEM((cz, 2 * nbc // cz, nr), F32),
            dma((nb + 3,)),
            dma((ny,)),
            dma((2, nb)),
            dma((2, nb)),
            dma((2, nx)),
            dma((2, nx)),
            dma((2,)),
            dma((2,)),
            dma((cz,)),
            dma((cz,)),
            dma((cx * cy,)),
            dma((cx * cy,)),
            dma((cz,)),
            dma((cz,)),
        ],
        compiler_params=pltpu.CompilerParams(
            collective_id=0, has_side_effects=True, vmem_limit_bytes=63 * 2**20
        ),
        name="galerkin",
    )(resident_basis, block_basis, jacobian, volumes, cell_codes, phase_index)
    return ((sums[:nbc] * scale).T, (sums[nbc:] * scale).T)


def solution(mesh):
    return jax.shard_map(
        shards,
        mesh=mesh,
        in_specs=(
            P(None, None, "gx", "gy", "gz"),
            P(None, None, None, "gx", "gy", "gz"),
            P(None, None, None, "gx", "gy", "gz"),
            P("gx", "gy", "gz"),
            P("gx", "gy", "gz"),
            P(),
        ),
        out_specs=(P(), P()),
        check_vma=False,
    )
```

time: 81.3 us -> 67.2 us (0.83)
  Pallas kernels: 76.6 us -> 64.2 us
  local copies, waits for them, and re-layouts: 3.23 us -> 0 us
  other arithmetic: 0 us -> 1.53 us
    pallas_call x1, Pallas kernels: 76.6 us -> 64.2 us  [shards(): pl.pallas_call(kernel, out_shape=jax.ShapeDtypeStruct((2 * nbc, nr), F32)...]
    pallas_call x2 -> x0, local copies, waits for them, and re-layouts: 3.23 us -> none  [shards(): pl.pallas_call(functools.partial(kernel, scale), out_shape=(out, out), in...]
    transpose x0 -> x1, other arithmetic: none -> 1.53 us  [shards(): return ((sums[:nbc] * scale).T, (sums[nbc:] * scale).T)]
where the time goes in v2:
time: 67.2 us; the launch traced here: 67 us
  Pallas kernels  64.2 us (96%)
  other arithmetic  1.53 us (2%)
  between operations  1.29 us (2%)
    pallas_call x1, Pallas kernels, shards(): pl.pallas_call(kernel, out_shape=jax.ShapeDtypeStruct((2 * nbc, nr), F32)...  64.2 us
    transpose x1, other arithmetic, shards(): return ((sums[:nbc] * scale).T, (sums[nbc:] * scale).T)  1.53 us

profile of v2, /device:TPU:1, one launch (start us, length us, event | category | flops | bytes accessed | tf_op | source)
XLA Modules:
  0.0 67.0 jit_solution(11493906835608382947)
XLA Ops:
  1.3 64.2 %galerkin.1 = f32[128,256]{1,0:T(8,128)} custom-call(bf16[5,256,4,8,256]{4,3,2,1,0:T(8,128)(2,1)} %basis_hbm.1, bf16[2,5,32,4,8,256]{5,4,3,2,1,0:T(8,128)(2,1)} %block_hbm.1, bf16[7,5,5,4,8,256]{5,4,3,2,1,0:T(8,128)(2,1)} %jac_hbm.1, f32[4,8,256]{2,1,0:T(8,128)} %vol_hbm.1, s32[4,8,256]{2,1,0:T(8,128)} %codes_hbm.1, s32[1]{0:T(128)S(6)} %copy.8.phase_ref), custom_call_target="tpu_custom_call" | custom-call | tf_op jit(solution)/shard_map/galerkin/pallas_call | solution.py:428
  65.5 1.5 %multiply_bitcast_fusion = (f32[256,64]{0,1:T(8,128)}, f32[256,64]{0,1:T(8,128)}) fusion(f32[128,256]{1,0:T(8,128)} %galerkin.1), kind=kLoop, calls=%fused_computation | loop fusion | flops 32768 | bytes 262144 | tf_op jit(solution)/shard_map/transpose | solution.py:478

commit v3 on v2

--- a/solution.py
+++ b/solution.py
@@ -38,9 +38,9 @@
     col_out,
     col_in,
     col,
-    partial,
     done_a,
     done_b,
+    done_c,
     total,
     sums,
     gather1,
@@ -136,12 +136,11 @@
         basis_copy(order[0], i).start()
         return carry
 
+    pl.semaphore_wait(barrier, cz - 1 + plane - 1)
+    for part in range(nb):
+        for side in range(2):
+            face_copy(side, part).start()
     for b in range(nb):
-        if b == nb - 1:
-            pl.semaphore_wait(barrier, cz - 1 + plane - 1)
-            for part in range(nb):
-                for side in range(2):
-                    face_copy(side, part).start()
         block_copies[b].wait()
         if b == nb - 1:
             lax.fori_loop(0, ny, first_basis, 0)
@@ -250,8 +249,8 @@
                 for s, xn in ((1, x - 1), (2, x + 1)):
                     if 0 <= xn < nx:
                         add(s, f, ext[xn, 1 + y, f, at, lanes])
-                    elif side == 1 or b == 0:
-                        add(s, f, face[b if side else 0, y, f, :, lanes])
+                    else:
+                        add(s, f, face[side, y, f, :, lanes])
                 add(3, f, ext[x, y, f, at, lanes])
                 add(4, f, ext[x, 2 + y, f, at, lanes])
                 if half == 0:
@@ -270,7 +269,7 @@
                 store(b, g, lanes, acc[g])
 
     total[...] = jnp.zeros_like(total)
-    for done in (done_a, done_b):
+    for done in (done_a, done_c):
         for g in range(nf):
             done[g, ny] = jnp.zeros(done.shape[2:], BF16)
 
@@ -279,34 +278,27 @@
         right = jnp.concatenate([done[g, row] for g in range(nf)], axis=1)
         total[...] += lax.dot_general(left, right, NT, preferred_element_type=F32)
 
-    def load_face(side, b, slot):
+    def load_face(side, b):
         face_copy(side, b).wait()
 
         def one(f, carry):
             rows = jnp.swapaxes(face_nat[side, b, f], 0, 1).astype(F32)
-            face[slot, :, f] = rows * keep_x[side]
+            face[side, :, f] = rows * keep_x[side]
             return carry
 
         lax.fori_loop(0, nf, one, 0)
 
-    def finish(y):
-        for half in range(halves):
-            lanes = pl.ds(half * 128, 128)
-            acc = [partial[y, g, :, lanes] for g in range(nf)]
-            for f in range(nf):
-                values = face[2, y, f, :, lanes]
-                for g in range(nf):
-                    acc[g] = acc[g] + jac[0, y, pl.ds((nf + f) * nf + g, 1), lanes] * values
-            for g in range(nf):
-                done_a[g, y, pl.ds(nc, nc), lanes] = acc[g].astype(BF16)
-
-    swaps = (swapped_a, swapped_b)
-    dones = (done_a, done_b)
-    for n, x in enumerate(order):
-        done = dones[n % 2]
-        side = 0 if x == 0 else 1 if x == nx - 1 else None
+    outer = ((0, 0, done_a), (nx - 1, 1, done_c))
+    steps = (
+        ((1, None, done_a, range(nb)),),
+        ((2, None, done_b, range(nb)),),
+        tuple(layer + ((0,),) for layer in outer),
+        tuple(layer + ((1,),) for layer in outer),
+    )
+    for n, layers in enumerate(steps):
         if n == 2:
-            load_face(0, 0, 0)
+            for side in range(2):
+                load_face(side, 0)
         if n == 3:
 
             def late(i, carry):
@@ -314,49 +306,52 @@
                 return carry
 
             lax.fori_loop(0, ny, late, 0)
-            load_face(1, 0, 0)
-            load_face(0, 1, 2)
-            load_face(1, 1, 1)
-
-        def row(i, carry, n=n, x=x, side=side, done=done):
+            for side in range(2):
+                load_face(side, 1)
+
+        def row(i, carry, n=n, layers=layers):
             y = (i + 1) % ny
 
-            @pl.when(i == ny - 2)
-            def _():
-                for t in range(2):
-                    rim_copy(t, x).wait()
-
-                    def turn(f, carry, t=t):
-                        re = rim_in[t, x, f, :nc].astype(F32)
-                        im = rim_in[t, x, f, nc:].astype(F32)
-                        ext[x, t * (ny + 1), f, :nc] = turn_c[t] * re + turn_s[t] * im
-                        ext[x, t * (ny + 1), f, nc:] = turn_c[t] * im - turn_s[t] * re
-                        return carry
-
-                    lax.fori_loop(0, nf, turn, 0)
-
-            def store(b, g, lanes, value):
-                if side == 0 and b == 1:
-                    partial[y, g, :, lanes] = value
-                else:
-                    done[g, y, pl.ds(b * nc, nc), lanes] = value.astype(BF16)
+            if n < 3:
+
+                @pl.when(i == ny - 2)
+                def _():
+                    for x, _side, _done, _parts in layers:
+                        for t in range(2):
+                            rim_copy(t, x).wait()
+
+                            def turn(f, carry, x=x, t=t):
+                                re = rim_in[t, x, f, :nc].astype(F32)
+                                im = rim_in[t, x, f, nc:].astype(F32)
+                                ext[x, t * (ny + 1), f, :nc] = turn_c[t] * re + turn_s[t] * im
+                                ext[x, t * (ny + 1), f, nc:] = turn_c[t] * im - turn_s[t] * re
+                                return carry
+
+                            lax.fori_loop(0, nf, turn, 0)
 
             if n == 2:
                 swap(n, i)
-            if n == 1 or n == 2:
-                project(i, swaps[1 - n % 2], dones[1 - n % 2], i)
+            if n == 1:
+                project(i, swapped_a, done_a, i)
+            if n == 2:
+                project(i, swapped_b, done_b, i)
             if n == 3:
-                project((y + ny - 1) % ny, swapped_a, done_a, jnp.where(i == 0, ny, (y + ny - 1) % ny))
-                project((y + ny - 1) % ny, swapped_b, done_b, jnp.where(i == 0, ny, (y + ny - 1) % ny))
-                finish(y)
-            for b in range(nb):
-                stencil(x, y, b, side, done, store)
+                before = (y + ny - 1) % ny
+                project(before, swapped_a, done_a, jnp.where(i == 0, ny, before))
+                project(before, swapped_b, done_c, jnp.where(i == 0, ny, before))
+            for x, side, done, parts in layers:
+
+                def store(b, g, lanes, value, done=done):
+                    done[g, y, pl.ds(b * nc, nc), lanes] = value.astype(BF16)
+
+                for b in parts:
+                    stencil(x, y, b, side, done, store)
             return carry
 
         lax.fori_loop(0, ny, row, 0)
 
     project(0, swapped_a, done_a, 0)
-    project(0, swapped_b, done_b, 0)
+    project(0, swapped_b, done_c, 0)
 
     sums[...] = total[...].T
     chunk = sums.shape[0] // cz
@@ -372,7 +367,8 @@
             device_id_type=MESH,
         )
 
-    for d in range(1, cz):
+    far_line = sorted(range(1, cz), key=lambda d: -min(d, cz - d))
+    for d in far_line:
         copy1(d).start()
     own = sums[pl.ds(pl.multiple_of(iz * chunk, chunk), chunk)]
     for d in range(1, cz):
@@ -386,11 +382,15 @@
             dst_ref=gather2.at[me2],
             send_sem=s2_sem.at[d],
             recv_sem=r2_sem.at[d],
-            device_id=in_plane((me2 + d) % plane),
-            device_id_type=MESH,
-        )
-
-    for d in range(1, plane):
+            device_id=((ix + d // cy) % cx, (iy + d % cy) % cy, iz),
+            device_id_type=MESH,
+        )
+
+    far_plane = sorted(
+        range(1, plane),
+        key=lambda d: -(min(d // cy, cx - d // cy) + min(d % cy, cy - d % cy)),
+    )
+    for d in far_plane:
         copy2(d).start()
     for d in range(1, plane):
         copy2(d).wait()
@@ -409,7 +409,7 @@
             device_id_type=MESH,
         )
 
-    for d in range(1, cz):
+    for d in far_line:
         copy3(d).start()
     for d in range(1, cz):
         copy3(d).wait()
@@ -441,13 +441,13 @@
             pltpu.VMEM((nf, ny, nr, nz), BF16),
             pltpu.VMEM((nf, ny, nr, nz), BF16),
             pltpu.VMEM((2, nb, nf, nc, ny, nz), BF16),
-            pltpu.VMEM((3, ny, nf, nc, nz), F32),
+            pltpu.VMEM((2, ny, nf, nc, nz), F32),
             pltpu.VMEM((2, nx, nf, nbc, nz), BF16),
             pltpu.VMEM((2, nx, nf, nbc, nz), BF16),
             pltpu.VMEM((2, nf, nbc, 128), BF16),
             pltpu.VMEM((2, nf, nbc, 128), BF16),
             pltpu.VMEM((2, nf, nbc, 128), F32),
-            pltpu.VMEM((ny, nf, nc, nz), F32),
+            pltpu.VMEM((nf, ny + 1, 2 * nbc, nz), BF16),
             pltpu.VMEM((nf, ny + 1, 2 * nbc, nz), BF16),
             pltpu.VMEM((nf, ny + 1, 2 * nbc, nz), BF16),
             pltpu.VMEM((nr, 2 * nbc), F32),

time: 67.2 us -> 67.3 us (level)
  no operation moved by 1% of the time
where the time goes in v3:
time: 67.3 us; the launch traced here: 67.2 us
  Pallas kernels  64.3 us (96%)
  other arithmetic  1.53 us (2%)
  between operations  1.29 us (2%)
    pallas_call x1, Pallas kernels, shards(): pl.pallas_call(kernel, out_shape=jax.ShapeDtypeStruct((2 * nbc, nr), F32)...  64.3 us
    transpose x1, other arithmetic, shards(): return ((sums[:nbc] * scale).T, (sums[nbc:] * scale).T)  1.53 us

profile of v3, /device:TPU:1, one launch (start us, length us, event | category | flops | bytes accessed | tf_op | source)
XLA Modules:
  0.0 67.2 jit_solution(6831422912713542853)
XLA Ops:
  1.3 64.3 %galerkin.1 = f32[128,256]{1,0:T(8,128)} custom-call(bf16[5,256,4,8,256]{4,3,2,1,0:T(8,128)(2,1)} %basis_hbm.1, bf16[2,5,32,4,8,256]{5,4,3,2,1,0:T(8,128)(2,1)} %block_hbm.1, bf16[7,5,5,4,8,256]{5,4,3,2,1,0:T(8,128)(2,1)} %jac_hbm.1, f32[4,8,256]{2,1,0:T(8,128)} %vol_hbm.1, s32[4,8,256]{2,1,0:T(8,128)} %codes_hbm.1, s32[1]{0:T(128)S(6)} %copy.8.phase_ref), custom_call_target="tpu_custom_call" | custom-call | tf_op jit(solution)/shard_map/galerkin/pallas_call | solution.py:428
  65.6 1.5 %multiply_bitcast_fusion = (f32[256,64]{0,1:T(8,128)}, f32[256,64]{0,1:T(8,128)}) fusion(f32[128,256]{1,0:T(8,128)} %galerkin.1), kind=kLoop, calls=%fused_computation | loop fusion | flops 32768 | bytes 262144 | tf_op jit(solution)/shard_map/transpose | solution.py:478
